TPU v7x, 32 devices: a whole 2x2x4 slice. The times are simulated.
32 devices in a mesh: tile: 8 (over z, core), view: 4 (over y, x).
Axes of the slice: x: 2, y: 2, z: 4, core: 2. Of those that a mesh axis runs over, the one named last changes fastest.
Arguments:
- estimate: float32 [128, 128, 256], P('tile', 'view'), may hold values from 0.5 to 2
- observed: float32 [4, 8, 26, 128, 256], P('view', 'tile'), may hold values from 0.25 to 4
- psf: float32 [12, 3, 11], replicated, may hold values from 0.1 to 1
- cover: int32 [8, 4], replicated, may hold values from 0 to 12, as said below
- offsets: int32 [8, 4], replicated, may hold values from -5 to 5
Outputs:
- updated: float32 [128, 128, 256], P('tile', 'view')
Inputs may be any that keep to these rules, and one draw needn't show every extreme that they name: `cover`: slot 0 of every block holds a view; slot 1 of block 0 is empty; other slots are empty with probability 0.4.
All inputs are finite; a program needn't handle non-finite values.
Results may differ from a plain program's by a relative error of at most 0.0003.
Values sent between devices are 32-bit elements; how exact they have to be, the bound alone decides.
A program may use at most 64 MiB of HBM per device.

v0:
```python
import jax
import jax.numpy as jnp
from jax import lax
from jax.sharding import PartitionSpec as P

ITERS = 2


def padded(cells, sides, width):
    for axis, dim in sides:
        count = lax.axis_size(axis)
        ends = count - 1
        head = lax.slice_in_dim(cells, 0, width, axis=dim)
        tail = lax.slice_in_dim(cells, cells.shape[dim] - width, cells.shape[dim], axis=dim)
        cells = jnp.concatenate(
            [
                lax.ppermute(tail, axis, [(i, (i + 1) % count) for i in range(ends)]),
                cells,
                lax.ppermute(head, axis, [((i + 1) % count, i) for i in range(ends)]),
            ],
            axis=dim,
        )
    return cells


def band_matrix(taps, rows, cols, z_offset, limit):
    radius = taps.shape[0] // 2
    offset = cols[None, :] - rows[:, None] - z_offset + radius
    inside = (cols[None, :] >= 0) & (cols[None, :] < limit)
    tap_index = jnp.arange(taps.shape[0], dtype=jnp.int32)
    weight = jnp.sum(jnp.where(offset[:, :, None] == tap_index, taps, 0.0), axis=2)
    weight = jnp.where(inside, weight, 0.0)
    return weight / jnp.sum(weight, axis=1, keepdims=True)


def view_kernels(psf, view_id):
    clipped = jnp.minimum(view_id, psf.shape[0] - 1)
    select = (jnp.arange(psf.shape[0], dtype=jnp.int32) == clipped).astype(psf.dtype)
    return jnp.sum(psf * select[:, None, None], axis=0)


def slot_back(extended, view_data, kernels, z_offset, first_row, total_rows, tile_rows):
    radius = kernels.shape[1] // 2
    exact = lax.Precision.HIGHEST
    rows = first_row - radius + jnp.arange(tile_rows + 2 * radius, dtype=jnp.int32)
    cols = first_row - 2 * radius + jnp.arange(tile_rows + 4 * radius, dtype=jnp.int32)
    x_weights = band_matrix(kernels[0], rows, cols, 0, total_rows)
    y_cells = jnp.arange(extended.shape[1], dtype=jnp.int32)
    z_cells = jnp.arange(extended.shape[2], dtype=jnp.int32)
    y_weights = band_matrix(kernels[1], y_cells, y_cells, 0, extended.shape[1])
    z_weights = band_matrix(kernels[2], z_cells, z_cells, z_offset, extended.shape[2])
    blurred = jnp.einsum("ij,jyz->iyz", x_weights, extended, precision=exact)
    blurred = jnp.einsum("yw,iwz->iyz", y_weights, blurred, precision=exact)
    blurred = jnp.einsum("iyw,zw->iyz", blurred, z_weights, precision=exact)
    in_range = ((rows >= 0) & (rows < total_rows)).astype(blurred.dtype)
    quotient = in_range[:, None, None] * view_data / blurred
    interior = x_weights[:, 2 * radius : 2 * radius + tile_rows]
    back_blur = jnp.einsum("ri,ryz->iyz", interior, quotient, precision=exact)
    back_blur = jnp.einsum("wy,iwz->iyz", y_weights, back_blur, precision=exact)
    back_blur = jnp.einsum("iyw,wz->iyz", back_blur, z_weights, precision=exact)
    return back_blur


def per_device(estimate, observed, psf, cover, offsets):
    tile_rows = estimate.shape[0]
    share_cols = estimate.shape[1]
    views_all = psf.shape[0]
    radius = psf.shape[2] // 2
    tile_index = lax.axis_index("tile")
    slot_index = lax.axis_index("view")
    total_rows = tile_rows * lax.axis_size("tile")
    first_row = tile_index * tile_rows
    cover_row = lax.dynamic_index_in_dim(cover, tile_index, 0, keepdims=False)
    view_id = lax.dynamic_index_in_dim(cover_row, slot_index, 0, keepdims=False)
    offset_row = lax.dynamic_index_in_dim(offsets, tile_index, 0, keepdims=False)
    z_offset = lax.dynamic_index_in_dim(offset_row, slot_index, 0, keepdims=False)
    kernels = view_kernels(psf, view_id)
    view_data = observed[0, 0]
    present = (view_id < views_all).astype(jnp.float32)
    coverage = jnp.sum((cover_row < views_all).astype(jnp.float32))
    whole_tile = lax.all_gather(estimate, "view", axis=1, tiled=True)
    extended = padded(whole_tile, (("tile", 0),), 2 * radius)
    current = extended[2 * radius : 2 * radius + tile_rows]
    for sweep_index in range(ITERS):
        if sweep_index > 0:
            extended = padded(current, (("tile", 0),), 2 * radius)
        summed = lax.psum(
            present
            * slot_back(extended, view_data, kernels, z_offset, first_row, total_rows, tile_rows),
            "view",
        )
        current = current * summed / coverage
    first_col = slot_index * share_cols
    return lax.dynamic_slice_in_dim(current, first_col, share_cols, 1)


def solution(mesh):
    placed = (P("tile", "view", None), P("view", "tile", None, None, None), P(), P(), P())
    return jax.shard_map(
        per_device, mesh=mesh, in_specs=placed, out_specs=P("tile", "view", None), check_vma=False
    )
```

profile of v0, /device:TPU:9, one launch (start us, length us, event | category | flops | bytes accessed | tf_op | source)
XLA Modules:
  0.0 312.2 jit_solution(70440127649699348)
XLA Ops:
  13.8 31.9 %all-gather.2.cloned.1.call-done = f32[16,128,256]{2,0,1:T(8,128)} async-done(((f32[16,32,256]{2,0,1:T(8,128)}), f32[16,128,256]{2,0,1:T(8,128)}) %all-gather.2.cloned.1.call-update) | async-done | bytes 2097168 | tf_op jit(solution)/shard_map/all_gather | solution.py:81
  45.7 2.6 fusion.54
  49.9 2.6 collective-permute-start.1
  52.5 3.3 %collective-permute-start = (f32[10,128,256]{2,1,0:T(8,128)S(1)}, f32[10,128,256]{2,1,0:T(8,128)S(1)}, u32[]{:S(2)}, u32[]{:S(2)}) collective-permute-start(f32[10,128,256]{2,1,0:T(8,128)S(1)} %copy.62), channel_id=1, source_target_pairs={{0,4},{4,8},{8,12},{12,16},{16,20},{20,24},{24,28},{1,5},{5,9},{9,... | collective-permute-start | bytes 3932168 | tf_op jit(solution)/shard_map/ppermute | solution.py:17
  57.5 11.6 %collective-permute-done.1 = f32[10,128,256]{2,1,0:T(8,128)S(1)} collective-permute-done((f32[10,128,256]{2,1,0:T(8,128)S(1)}, f32[10,128,256]{2,1,0:T(8,128)S(1)}, u32[]{:S(2)}, u32[]{:S(2)}) %collective-permute-start.1) | collective-permute-done | bytes 1310752 | tf_op jit(solution)/shard_map/ppermute | solution.py:19
  71.5 4.4 %fusion = f32[26,128,256]{2,0,1:T(8,128)S(1)} fusion(f32[10,128,256]{2,0,1:T(8,128)S(1)} %copy.65, f32[16,128,256]{2,0,1:T(8,128)S(1)} %copy-done, f32[10,128,256]{2,0,1:T(8,128)S(1)} %copy.64, f32[26,36]{1,0:T(8,128)S(1)} %select_divide_fusion.2), kind=kOutput, calls=%fused_computation | convolution fusion | flops 370409472 | bytes 8130208 | tf_op jit(solution)/shard_map/ij,jyz->iyz/dot_general | solution.py:52
  76.0 7.5 %fusion.18 = f32[26,256,128]{2,1,0:T(8,128)S(1)} fusion(f32[26,128,256]{2,0,1:T(8,128)S(1)} %fusion, f32[128,128]{1,0:T(8,128)S(1)} %select_reduce_fusion.1, f32[128]{0:T(128)S(1)} %select_reduce_fusion.4, pred[128]{0:T(512)(128)(4,1)S(1)} %iota_compare_fusion.4), kind=kOutput, calls=%fused_computation.20 | convolution fusion | flops 1308655616 | bytes 6881920 | tf_op jit(solution)/shard_map/yw,iwz->iyz/dot_general | solution.py:53
  83.4 6.4 %fusion.21 = f32[26,128,256]{2,1,0:T(8,128)S(1)} fusion(f32[1,1,26,128,256]{4,3,2,1,0:T(8,128)S(1)} %copy-done.3, f32[26,256,128]{2,1,0:T(8,128)S(1)} %fusion.18, f32[26]{0:T(128)S(1)} %and_convert_fusion, f32[256,256]{1,0:T(8,128)S(1)} %select_reduce_fusion, f32[256]{0:T(256)S(1)} %select_reduce_fusion.2, pred[256]{0:T(512)(128)(4,1)S(1)} %iota_compare_fusion.3), kind=kOutput, calls=%fused_computation.23 | convolution fusion | flops 2619080704 | bytes 10487144 | tf_op jit(solution)/shard_map/iyw,zw->iyz/dot_general | solution.py:54
  89.8 4.1 %fusion.10 = f32[16,128,256]{2,0,1:T(8,128)S(1)} fusion(f32[26,128,256]{2,1,0:T(8,128)S(1)} %fusion.21, f32[26,36]{1,0:T(8,128)S(1)} %select_divide_fusion.2), kind=kOutput, calls=%fused_computation.11 | convolution fusion | flops 163577856 | bytes 5508768 | tf_op jit(solution)/shard_map/ri,ryz->iyz/dot_general | solution.py:58
  93.9 4.5 %fusion.29 = f32[16,256,128]{2,1,0:T(8,128)S(1)} fusion(f32[16,128,256]{2,0,1:T(8,128)S(1)} %fusion.10, f32[128,128]{1,0:T(8,128)S(1)} %select_reduce_fusion.1, f32[128]{0:T(128)S(1)} %select_reduce_fusion.4, pred[128]{0:T(512)(128)(4,1)S(1)} %iota_compare_fusion.4), kind=kOutput, calls=%fused_computation.34 | convolution fusion | flops 805339136 | bytes 4260480 | tf_op jit(solution)/shard_map/wy,iwz->iyz/dot_general | solution.py:59
  98.4 4.9 %fusion.35 = f32[16,128,256]{2,1,0:T(8,128)} fusion(f32[16,256,128]{2,1,0:T(8,128)S(1)} %fusion.29, f32[]{:T(128)} %bitcast, f32[256,256]{1,0:T(8,128)S(1)} %select_reduce_fusion, f32[256]{0:T(256)S(1)} %select_reduce_fusion.2, pred[256]{0:T(512)(128)(4,1)S(1)} %iota_compare_fusion.3), kind=kOutput, calls=%fused_computation.36 | convolution fusion | flops 1611268096 | bytes 4457732 | tf_op jit(solution)/shard_map/iyw,wz->iyz/dot_general | solution.py:60
  104.7 68.5 %all-reduce.3.cloned.1.call-done = f32[16,128,256]{2,1,0:T(8,128)} async-done(((f32[16,128,256]{2,1,0:T(8,128)}), f32[16,128,256]{2,1,0:T(8,128)}) %all-reduce.3.cloned.1.call-update) | async-done | bytes 2097168 | tf_op jit(solution)/shard_map/psum | solution.py:87
  173.2 3.5 %fusion.28 = f32[16,128,256]{2,1,0:T(8,128)S(1)} fusion(f32[16,128,256]{2,1,0:T(8,128)} %all-reduce.3.cloned.1.call-done, f32[16,128,256]{2,0,1:T(8,128)S(1)} %copy-done, f32[]{:T(128)} %convert_reduce_fusion), kind=kLoop, calls=%fused_computation.33 | loop fusion | flops 1048576 | bytes 6291460 | tf_op jit(solution)/shard_map/div | solution.py:92
  177.0 3.7 %collective-permute-start.2 = (f32[10,128,256]{2,1,0:T(8,128)S(1)}, f32[10,128,256]{2,1,0:T(8,128)S(1)}, u32[]{:S(2)}, u32[]{:S(2)}) collective-permute-start(f32[10,128,256]{2,1,0:T(8,128)S(1)} %get-tuple-element.8), channel_id=1, source_target_pairs={{0,4},{4,8},{8,12},{12,16},{16,20},{20,24},{24,28},{1,5},{5,9},{9,... | collective-permute-start | bytes 3932168 | tf_op jit(solution)/shard_map/ppermute | solution.py:17
  182.8 12.4 %collective-permute-done.2 = f32[10,128,256]{2,1,0:T(8,128)S(1)} collective-permute-done((f32[10,128,256]{2,1,0:T(8,128)S(1)}, f32[10,128,256]{2,1,0:T(8,128)S(1)}, u32[]{:S(2)}, u32[]{:S(2)}) %collective-permute-start.2) | collective-permute-done | bytes 1310752 | tf_op jit(solution)/shard_map/ppermute | solution.py:17
  195.2 4.4 %collective-permute-done.3 = f32[10,128,256]{2,1,0:T(8,128)S(1)} collective-permute-done((f32[10,128,256]{2,1,0:T(8,128)S(1)}, f32[10,128,256]{2,1,0:T(8,128)S(1)}, u32[]{:S(2)}, u32[]{:S(2)}) %collective-permute-start.3) | collective-permute-done | bytes 1310752 | tf_op jit(solution)/shard_map/ppermute | solution.py:19
  200.1 7.1 %fusion.6 = f32[26,128,256]{2,0,1:T(8,128)S(1)} fusion(f32[36,128,256]{2,1,0:T(8,128)S(1)} %pad_maximum_fusion, f32[26,36]{1,0:T(8,128)S(1)} %select_divide_fusion.2), kind=kOutput, calls=%fused_computation.6 | convolution fusion | flops 368050176 | bytes 8130208 | tf_op jit(solution)/shard_map/ij,jyz->iyz/dot_general | solution.py:52
  207.2 7.3 %fusion.16 = f32[26,256,128]{2,1,0:T(8,128)S(1)} fusion(f32[26,128,256]{2,0,1:T(8,128)S(1)} %fusion.6, f32[128,128]{1,0:T(8,128)S(1)} %select_reduce_fusion.1, f32[128]{0:T(128)S(1)} %select_reduce_fusion.4, pred[128]{0:T(512)(128)(4,1)S(1)} %iota_compare_fusion.4), kind=kOutput, calls=%fused_computation.18 | convolution fusion | flops 1308655616 | bytes 6881920 | tf_op jit(solution)/shard_map/yw,iwz->iyz/dot_general | solution.py:53
  214.5 6.3 %fusion.20 = f32[26,128,256]{2,1,0:T(8,128)S(1)} fusion(f32[1,1,26,128,256]{4,3,2,1,0:T(8,128)S(1)} %copy-done.4, f32[26,256,128]{2,1,0:T(8,128)S(1)} %fusion.16, f32[26]{0:T(128)S(1)} %and_convert_fusion, f32[256,256]{1,0:T(8,128)S(1)} %select_reduce_fusion, f32[256]{0:T(256)S(1)} %select_reduce_fusion.2, pred[256]{0:T(512)(128)(4,1)S(1)} %iota_compare_fusion.3), kind=kOutput, calls=%fused_computation.22 | convolution fusion | flops 2619080704 | bytes 10487144 | tf_op jit(solution)/shard_map/iyw,zw->iyz/dot_general | solution.py:54
  220.9 4.2 %fusion.8 = f32[16,128,256]{2,0,1:T(8,128)S(1)} fusion(f32[26,128,256]{2,1,0:T(8,128)S(1)} %fusion.20, f32[26,36]{1,0:T(8,128)S(1)} %select_divide_fusion.2), kind=kOutput, calls=%fused_computation.9 | convolution fusion | flops 163577856 | bytes 5508768 | tf_op jit(solution)/shard_map/ri,ryz->iyz/dot_general | solution.py:58
  225.1 4.3 %fusion.26 = f32[16,256,128]{2,1,0:T(8,128)S(1)} fusion(f32[16,128,256]{2,0,1:T(8,128)S(1)} %fusion.8, f32[128,128]{1,0:T(8,128)S(1)} %select_reduce_fusion.1, f32[128]{0:T(128)S(1)} %select_reduce_fusion.4, pred[128]{0:T(512)(128)(4,1)S(1)} %iota_compare_fusion.4), kind=kOutput, calls=%fused_computation.30 | convolution fusion | flops 805339136 | bytes 4260480 | tf_op jit(solution)/shard_map/wy,iwz->iyz/dot_general | solution.py:59
  229.4 5.0 %fusion.38 = f32[16,128,256]{2,1,0:T(8,128)} fusion(f32[16,256,128]{2,1,0:T(8,128)S(1)} %fusion.26, f32[]{:T(128)} %bitcast, f32[256,256]{1,0:T(8,128)S(1)} %select_reduce_fusion, f32[256]{0:T(256)S(1)} %select_reduce_fusion.2, pred[256]{0:T(512)(128)(4,1)S(1)} %iota_compare_fusion.3), kind=kOutput, calls=%fused_computation.37 | convolution fusion | flops 1611268096 | bytes 4457732 | tf_op jit(solution)/shard_map/iyw,wz->iyz/dot_general | solution.py:60
  234.4 68.4 %all-reduce.5.cloned.1.call-done = f32[16,128,256]{2,1,0:T(8,128)} async-done(((f32[16,128,256]{2,1,0:T(8,128)}), f32[16,128,256]{2,1,0:T(8,128)}) %all-reduce.5.cloned.1.call-update) | async-done | bytes 2097168 | tf_op jit(solution)/shard_map/psum | solution.py:87
  302.8 2.7 fusion.41
  (47 shorter events, 15.8 us)
Async XLA Ops:
  6.5 39.2 %all-gather.2.cloned.1.call-start = ((), (), s32[]{:S(2)}) async-start(), calls=%async_computation | async-start | bytes 2621440 | tf_op jit(solution)/shard_map/all_gather | solution.py:81
  8.7 164.5 %all-reduce.3.cloned.1.call-start = ((), (), s32[]{:S(2)}) async-start(), calls=%async_computation.1 | async-start | bytes 4194304 | tf_op jit(solution)/shard_map/psum | solution.py:87
  49.9 19.3 %collective-permute-start.1 = (f32[10,128,256]{2,1,0:T(8,128)S(1)}, f32[10,128,256]{2,1,0:T(8,128)S(1)}, u32[]{:S(2)}, u32[]{:S(2)}) collective-permute-start(f32[10,128,256]{2,1,0:T(8,128)S(1)} %copy.63), channel_id=1, source_target_pairs={{4,0},{8,4},{12,8},{16,12},{20,16},{24,20},{28,24},{5,1},{9,5},{13... | collective-permute-start | bytes 3932168 | tf_op jit(solution)/shard_map/ppermute | solution.py:19
  52.5 17.6 %collective-permute-start = (f32[10,128,256]{2,1,0:T(8,128)S(1)}, f32[10,128,256]{2,1,0:T(8,128)S(1)}, u32[]{:S(2)}, u32[]{:S(2)}) collective-permute-start(f32[10,128,256]{2,1,0:T(8,128)S(1)} %copy.62), channel_id=1, source_target_pairs={{0,4},{4,8},{8,12},{12,16},{16,20},{20,24},{24,28},{1,5},{5,9},{9,... | collective-permute-start | bytes 3932168 | tf_op jit(solution)/shard_map/ppermute | solution.py:17
  69.9 1.6 copy-start
  76.0 7.5 %copy-start.3 = (f32[1,1,26,128,256]{4,3,2,1,0:T(8,128)S(1)}, f32[1,1,26,128,256]{4,3,2,1,0:T(8,128)}, u32[]{:S(2)}) copy-start(f32[1,1,26,128,256]{4,3,2,1,0:T(8,128)} %param.6) | copy-start | bytes 10223620
  103.3 0.7 copy-start.2
  103.3 199.5 %all-reduce.5.cloned.1.call-start = ((), (), s32[]{:S(2)}) async-start(), calls=%async_computation.2 | async-start | bytes 4194304 | tf_op jit(solution)/shard_map/psum | solution.py:87
  176.7 22.9 %copy-start.1 = (f32[16,128,256]{2,1,0:T(8,128)}, f32[16,128,256]{2,1,0:T(8,128)S(1)}, u32[]{:S(2)}) copy-start(f32[16,128,256]{2,1,0:T(8,128)S(1)} %fusion.28) | copy-start | bytes 6291460
  177.0 18.2 %collective-permute-start.2 = (f32[10,128,256]{2,1,0:T(8,128)S(1)}, f32[10,128,256]{2,1,0:T(8,128)S(1)}, u32[]{:S(2)}, u32[]{:S(2)}) collective-permute-start(f32[10,128,256]{2,1,0:T(8,128)S(1)} %get-tuple-element.8), channel_id=1, source_target_pairs={{0,4},{4,8},{8,12},{12,16},{16,20},{20,24},{24,28},{1,5},{5,9},{9,... | collective-permute-start | bytes 3932168 | tf_op jit(solution)/shard_map/ppermute | solution.py:17
  180.6 18.9 %collective-permute-start.3 = (f32[10,128,256]{2,1,0:T(8,128)S(1)}, f32[10,128,256]{2,1,0:T(8,128)S(1)}, u32[]{:S(2)}, u32[]{:S(2)}) collective-permute-start(f32[10,128,256]{2,1,0:T(8,128)S(1)} %get-tuple-element.9), channel_id=1, source_target_pairs={{4,0},{8,4},{12,8},{16,12},{20,16},{24,20},{28,24},{5,1},{9,5},{13... | collective-permute-start | bytes 3932168 | tf_op jit(solution)/shard_map/ppermute | solution.py:19
  207.2 7.3 %copy-start.4 = (f32[1,1,26,128,256]{4,3,2,1,0:T(8,128)S(1)}, f32[1,1,26,128,256]{4,3,2,1,0:T(8,128)}, u32[]{:S(2)}) copy-start(f32[1,1,26,128,256]{4,3,2,1,0:T(8,128)} %param.6) | copy-start | bytes 10223620
Sparse Core Ops, SparseCore 0:
  9.2 36.4 all-gather.1
  103.4 69.6 all-reduce.2
  234.5 68.2 all-reduce.4
where the time goes:
time: 317 us; the launch traced here: 312 us
  waiting for transfers between devices  197 us (62%)
  matrix products  66 us (21%)
  between operations  14.8 us (5%)
  local copies, waits for them, and re-layouts  12.3 us (4%)
  starting transfers between devices  11.8 us (4%)
  other arithmetic  9.99 us (3%)
    psum x2, waiting for transfers between devices, per_device(): lax.psum(present * slot_back(extended, view_data, kernels, z_offset, firs...  137 us
    all_gather x1, waiting for transfers between devices, per_device(): whole_tile = lax.all_gather(estimate, 'view', axis=1, tiled=True)  31.9 us
    ppermute x2, waiting for transfers between devices, padded(): lax.ppermute(head, axis, [((i + 1) % count, i) for i in range(ends)])  16 us
    dot_general x2, matrix products, slot_back(): blurred = jnp.einsum('yw,iwz->iyz', y_weights, blurred, precision=exact)  14.8 us
    dot_general x2, matrix products, slot_back(): blurred = jnp.einsum('iyw,zw->iyz', blurred, z_weights, precision=exact)  12.7 us
    ppermute x2, waiting for transfers between devices, padded(): lax.ppermute(tail, axis, [(i, (i + 1) % count) for i in range(ends)])  12.5 us
    dot_general x2, matrix products, slot_back(): blurred = jnp.einsum('ij,jyz->iyz', x_weights, extended, precision=exact)  11.5 us
    dot_general x2, matrix products, slot_back(): back_blur = jnp.einsum('iyw,wz->iyz', back_blur, z_weights, precision=exact)  9.93 us
  transfers between devices with their start and end apart: 7, of which 7 were waited for; matrix products, arithmetic and copies ran while one was open for 2% of the time, Pallas kernels for 0%

commit v1 on v0

v1 whole, which is shorter than its diff:
```python
import functools

import jax
import jax.numpy as jnp
from jax import lax
from jax.experimental import pallas as pl
from jax.experimental.pallas import tpu as pltpu
from jax.sharding import PartitionSpec as P

ITERS = 2


def split(x):
    high = x.astype(jnp.bfloat16)
    low = (x - high.astype(jnp.float32)).astype(jnp.bfloat16)
    return high, low


def dot(a, b):
    return jnp.dot(a, b, preferred_element_type=jnp.float32)


def dot3(a, b):
    (ah, al), (bh, bl) = a, b
    return dot(ah, bh) + (dot(ah, bl) + dot(al, bh))


def kernel(
    tiles, slots, est, obs_hbm, psf, cover, offsets, out,
    cells, mid, obs, sent, got, own, wz, wzt, wy, wyt,
    obs_sem, gs, gr, hs, hr, rs, rr,
):
    t = lax.axis_index("tile")
    s = lax.axis_index("view")
    rows, share, nz = est.shape
    ny = mid.shape[1]
    views, _, taps = psf.shape
    rad = taps // 2
    wide = rows + 2 * rad
    has_prev, has_next = t > 0, t < tiles - 1

    def cols(d):
        return pl.ds(pl.multiple_of(lax.rem(s + slots - d, slots) * share, 8), share)

    def peer(d):
        return {"view": lax.rem(s + d, slots)}

    obs_copy = pltpu.make_async_copy(obs_hbm.at[0, 0], obs, obs_sem)
    obs_copy.start()

    barrier = pltpu.get_barrier_semaphore()
    for d in range(1, slots):
        pl.semaphore_signal(barrier, inc=1, device_id=peer(d), device_id_type=pl.DeviceIdType.MESH)

    @pl.when(has_prev)
    def _():
        pl.semaphore_signal(barrier, inc=1, device_id={"tile": t - 1}, device_id_type=pl.DeviceIdType.MESH)

    @pl.when(has_next)
    def _():
        pl.semaphore_signal(barrier, inc=1, device_id={"tile": t + 1}, device_id_type=pl.DeviceIdType.MESH)

    neighbours = has_prev.astype(jnp.int32) + has_next.astype(jnp.int32)
    pl.semaphore_wait(barrier, slots - 1 + neighbours)

    def gather(b, d):
        src = est if b == 0 else cells.at[b, pl.ds(2 * rad, rows), cols(0), :]
        return pltpu.make_async_remote_copy(
            src_ref=src,
            dst_ref=cells.at[b, pl.ds(2 * rad, rows), cols(0), :],
            send_sem=gs.at[b, d], recv_sem=gr.at[b, d],
            device_id=peer(d), device_id_type=pl.DeviceIdType.MESH,
        )

    def gather_in(b, d):
        block = cells.at[b, pl.ds(2 * rad, rows), cols(d), :]
        return pltpu.make_async_remote_copy(
            src_ref=block, dst_ref=block,
            send_sem=gs.at[b, d], recv_sem=gr.at[b, d],
            device_id=peer(d), device_id_type=pl.DeviceIdType.MESH,
        )

    def halo(b, d, up):
        first, to = (rows, 0) if up else (2 * rad, rows + 2 * rad)
        return pltpu.make_async_remote_copy(
            src_ref=cells.at[b, pl.ds(first, 2 * rad), cols(d), :],
            dst_ref=cells.at[b, pl.ds(to, 2 * rad), cols(d), :],
            send_sem=hs.at[b, d, int(up)], recv_sem=hr.at[b, d, int(up)],
            device_id={"tile": t + 1 if up else t - 1}, device_id_type=pl.DeviceIdType.MESH,
        )

    def halo_start(b, d):
        @pl.when(has_next)
        def _():
            halo(b, d, True).start()

        @pl.when(has_prev)
        def _():
            halo(b, d, False).start()

    def halo_wait(b, d):
        @pl.when(has_prev)
        def _():
            halo(b, d, True).wait_recv()

        @pl.when(has_next)
        def _():
            halo(b, d, False).wait_recv()

    def halo_sent(b, d):
        @pl.when(has_next)
        def _():
            halo(b, d, True).wait_send()

        @pl.when(has_prev)
        def _():
            halo(b, d, False).wait_send()

    def scatter(b, d):
        return pltpu.make_async_remote_copy(
            src_ref=sent.at[b, d - 1], dst_ref=got.at[b, d - 1],
            send_sem=rs.at[b, d], recv_sem=rr.at[b, d],
            device_id=peer(d), device_id_type=pl.DeviceIdType.MESH,
        )

    view = cover[t, s]
    clipped = jnp.minimum(view, views - 1)
    shift = offsets[t, s]
    count = jnp.float32(0.0)
    for d in range(slots):
        count = count + jnp.where(cover[t, d] < views, 1.0, 0.0)
    scale = jnp.where(view < views, 1.0, 0.0) / jnp.full((8, nz), count, jnp.float32)
    bx = [psf[clipped, 0, k] for k in range(taps)]

    def band(size, axis, offset, high, low, transposed):
        r = lax.broadcasted_iota(jnp.int32, (size, size), 1 if transposed else 0)
        c = lax.broadcasted_iota(jnp.int32, (size, size), 0 if transposed else 1)
        where = c - r - offset + rad
        weight = jnp.zeros((size, size), jnp.float32)
        for k in range(taps):
            weight = jnp.where(where == k, psf[clipped, axis, k], weight)
        h, l = split(weight)
        high[...] = h
        low[...] = l

    def forward(b, d):
        base = lax.rem(s + slots - d, slots) * share

        @pl.loop(0, share // 8)
        def _(i):
            at = pl.ds(pl.multiple_of(base + i * 8, 8), 8)
            x = [cells[b, j, at, :] for j in range(rows + 4 * rad)]
            sums = []
            for r in range(wide):
                total = bx[0] * x[r]
                for k in range(1, taps):
                    total = total + bx[k] * x[r + k]
                sums.append(total)
            data = split(jnp.concatenate(sums, axis=0))
            z = dot3(data, (wzt[0], wzt[1]))
            mid[:, at, :] = z.reshape(wide, 8, nz)

    def middle():
        @pl.loop(0, wide)
        def _(r):
            row = t * rows - rad + r
            inside = jnp.logical_and(row >= 0, row < tiles * rows)
            blurred = dot3((wy[0], wy[1]), split(mid[r]))
            quotient = jnp.where(inside, obs[r], 0.0) / blurred
            mid[r] = dot3((wyt[0], wyt[1]), split(quotient))

    def backward(d, put):
        base = lax.rem(s + d, slots) * share

        @pl.loop(0, share // 8)
        def _(i):
            at = pl.ds(pl.multiple_of(base + i * 8, 8), 8)
            q = [mid[j, at, :] for j in range(wide)]
            sums = []
            for r in range(rows):
                total = bx[0] * q[r + 2 * rad]
                for k in range(1, taps):
                    total = total + bx[k] * q[r + 2 * rad - k]
                sums.append(total)
            data = split(jnp.concatenate(sums, axis=0))
            z = dot3(data, (wz[0], wz[1])).reshape(rows, 8, nz) * scale[None]
            put(pl.ds(pl.multiple_of(i * 8, 8), 8), z)

    for b in range(ITERS):
        for d in range(1, slots):
            gather(b, d).start()
        if b == 0:
            cells[0, pl.ds(2 * rad, rows), cols(0), :] = est[...]
        halo_start(b, 0)

        @pl.when(jnp.logical_not(has_prev))
        def _():
            cells[b, pl.ds(0, 2 * rad), :, :] = jnp.zeros((2 * rad, ny, nz), jnp.float32)

        @pl.when(jnp.logical_not(has_next))
        def _():
            cells[b, pl.ds(rows + 2 * rad, 2 * rad), :, :] = jnp.zeros((2 * rad, ny, nz), jnp.float32)

        if b == 0:
            band(nz, 2, shift, wzt.at[0], wzt.at[1], True)
            band(nz, 2, shift, wz.at[0], wz.at[1], False)
            band(ny, 1, 0, wy.at[0], wy.at[1], False)
            band(ny, 1, 0, wyt.at[0], wyt.at[1], True)
        for d in range(1, slots + 1):
            if d < slots:
                gather_in(b, d).wait_recv()
                halo_start(b, d)
            halo_wait(b, d - 1)
            forward(b, d - 1)
        if b == 0:
            obs_copy.wait()
        middle()
        for d in range(1, slots):
            def put(at, z, d=d):
                sent[b, d - 1, :, at, :] = z

            backward(d, put)
            scatter(b, d).start()

        def keep(at, z):
            own[:, at, :] = z

        backward(0, keep)
        for d in range(1, slots):
            scatter(b, d).wait_recv()
        target = out if b == ITERS - 1 else None

        @pl.loop(0, rows)
        def _(r):
            total = own[r]
            for d in range(1, slots):
                total = total + got[b, d - 1, r]
            new = cells[b, 2 * rad + r, cols(0), :] * total
            if target is not None:
                out[r] = new
            else:
                cells[b + 1, 2 * rad + r, cols(0), :] = new

    for b in range(ITERS):
        for d in range(slots):
            if d:
                gather(b, d).wait_send()
                scatter(b, d).wait_send()
            halo_sent(b, d)


def per_device(tiles, slots, estimate, observed, psf, cover, offsets):
    rows, share, nz = estimate.shape
    wide, ny = observed.shape[2:4]
    f32, bf16, dma = jnp.float32, jnp.bfloat16, pltpu.SemaphoreType.DMA
    vmem = pl.BlockSpec(memory_space=pltpu.VMEM)
    smem = pl.BlockSpec(memory_space=pltpu.SMEM)
    return pl.pallas_call(
        functools.partial(kernel, tiles, slots),
        out_shape=jax.ShapeDtypeStruct(estimate.shape, f32),
        in_specs=[vmem, pl.BlockSpec(memory_space=pl.ANY), smem, smem, smem],
        out_specs=vmem,
        scratch_shapes=[
            pltpu.VMEM((ITERS, 2 * wide - rows, ny, nz), f32),
            pltpu.VMEM((wide, ny, nz), f32),
            pltpu.VMEM((wide, ny, nz), f32),
            pltpu.VMEM((ITERS, slots - 1, rows, share, nz), f32),
            pltpu.VMEM((ITERS, slots - 1, rows, share, nz), f32),
            pltpu.VMEM((rows, share, nz), f32),
            pltpu.VMEM((2, nz, nz), bf16),
            pltpu.VMEM((2, nz, nz), bf16),
            pltpu.VMEM((2, ny, ny), bf16),
            pltpu.VMEM((2, ny, ny), bf16),
            dma,
            dma((ITERS, slots)), dma((ITERS, slots)),
            dma((ITERS, slots, 2)), dma((ITERS, slots, 2)),
            dma((ITERS, slots)), dma((ITERS, slots)),
        ],
        compiler_params=pltpu.CompilerParams(
            collective_id=0, has_side_effects=True, vmem_limit_bytes=48 * 1024 * 1024
        ),
    )(estimate, observed, psf, cover, offsets)


def solution(mesh):
    placed = (P("tile", "view", None), P("view", "tile", None, None, None), P(), P(), P())
    return jax.shard_map(
        functools.partial(per_device, mesh.shape["tile"], mesh.shape["view"]),
        mesh=mesh, in_specs=placed, out_specs=P("tile", "view", None), check_vma=False,
    )
```

time: 317 us -> 150 us (0.47); the launches traced: 312 us -> 149 us
  waiting for transfers between devices: 197 us -> 0 us
  Pallas kernels: 0 us -> 143 us
  matrix products: 66 us -> 0 us
  between operations: 14.8 us -> 0.01 us
  starting transfers between devices: 11.8 us -> 0 us
  other arithmetic: 9.99 us -> 0 us
  local copies, waits for them, and re-layouts: 12.3 us -> 6.15 us
    pallas_call x0 -> x1, Pallas kernels: none -> 143 us  [per_device(): pl.pallas_call(functools.partial(kernel, tiles, slots), out_shape=jax.Sha...]
    psum x2 -> x0, waiting for transfers between devices: 137 us -> none  [per_device(): lax.psum(present * slot_back(extended, view_data, kernels, z_offset, firs...]
    dot_general x12 -> x0, matrix products: 66 us -> none  [the longest x2 14.8 us: slot_back(): blurred = jnp.einsum('yw,iwz->iyz', y_weights, blurred, precision=exact)]
    all_gather x1 -> x0, waiting for transfers between devices: 31.9 us -> none  [per_device(): whole_tile = lax.all_gather(estimate, 'view', axis=1, tiled=True)]
    ppermute x4 -> x0, waiting for transfers between devices: 28.5 us -> none  [the longest x2 16 us: padded(): lax.ppermute(head, axis, [((i + 1) % count, i) for i in range(ends)])]
    ppermute x4 -> x0, starting transfers between devices: 11.7 us -> none  [the longest x2 6.98 us: padded(): lax.ppermute(tail, axis, [(i, (i + 1) % count) for i in range(ends)])]
    div x3 -> x0, other arithmetic: 6.3 us -> none  [the longest x2 6.22 us: per_device(): current = current * summed / coverage]
    slice x5 -> x0, local copies, waits for them, and re-layouts: 4.64 us -> none  [the longest x3 3.66 us: padded(): lax.slice_in_dim(cells, cells.shape[dim] - width, cells.shape[dim], axis=...]
  transfers between devices with their start and end apart: 7 -> 0, of which waited for: 7 -> 0; matrix products, arithmetic and copies ran while one was open for 2% -> 0% of each run, Pallas kernels for 0% -> 0%
where the time goes in v1:
time: 150 us; the launch traced here: 149 us
  Pallas kernels  143 us (95%)
  local copies, waits for them, and re-layouts  6.15 us (4%)
    pallas_call x1, Pallas kernels, per_device(): pl.pallas_call(functools.partial(kernel, tiles, slots), out_shape=jax.Sha...  143 us
    unnamed x8, local copies, waits for them, and re-layouts  6.15 us

profile of v1, /device:TPU:9, one launch (start us, length us, event | category | flops | bytes accessed | tf_op | source)
XLA Modules:
  0.0 148.9 jit_solution(12390256498002309570)
XLA Ops:
  0.0 0.8 copy.7.cover
  0.8 0.8 copy.8.offsets
  1.5 0.8 copy.6.psf
  2.3 0.0 copy-start
  2.4 2.0 %copy-done = f32[1,1,26,128,256]{4,3,2,1,0:T(8,128)S(1)} copy-done((f32[1,1,26,128,256]{4,3,2,1,0:T(8,128)S(1)}, f32[1,1,26,128,256]{4,3,2,1,0:T(8,128)}, u32[]{:S(2)}) %copy-start) | copy-done | bytes 3407896
  4.3 0.0 copy-start.1
  4.3 1.0 copy-done.1
  5.4 142.8 %shard_map.55 = f32[16,32,256]{2,1,0:T(8,128)S(1)} custom-call(f32[16,32,256]{2,1,0:T(8,128)S(1)} %copy-done.1, f32[1,1,26,128,256]{4,3,2,1,0:T(8,128)S(1)} %copy-done, f32[12,3,11]{2,1,0:T(4,128)S(1)} %copy.6.psf, s32[8,4]{1,0:T(8,128)S(1)} %copy.7.cover, s32[8,4]{1,0:T(8,128)S(1)} %copy.8.offsets), custom_call_target="tpu_custom_call" | custom-call | tf_op jit(solution)/shard_map/pallas_call | solution.py:258
  148.1 0.8 copy.10
Async XLA Ops:
  2.3 2.0 %copy-start = (f32[1,1,26,128,256]{4,3,2,1,0:T(8,128)S(1)}, f32[1,1,26,128,256]{4,3,2,1,0:T(8,128)}, u32[]{:S(2)}) copy-start(f32[1,1,26,128,256]{4,3,2,1,0:T(8,128)} %obs_hbm.1) | copy-start | bytes 10223620
  4.3 1.0 copy-start.1

commit v2 on v1

--- a/solution.py
+++ b/solution.py
@@ -39,11 +39,21 @@
     wide = rows + 2 * rad
     has_prev, has_next = t > 0, t < tiles - 1
 
+    half = rows // 2
+    grid = slots == 4
+    around = (s, s + 1 - 2 * lax.rem(s, 2), lax.rem(s + 2, 4), 3 - s)
+
+    def source(d):
+        return around[d] if grid else lax.rem(s + slots - d, slots)
+
+    def goal(d):
+        return around[d] if grid else lax.rem(s + d, slots)
+
     def cols(d):
-        return pl.ds(pl.multiple_of(lax.rem(s + slots - d, slots) * share, 8), share)
+        return pl.ds(pl.multiple_of(source(d) * share, 8), share)
 
     def peer(d):
-        return {"view": lax.rem(s + d, slots)}
+        return {"view": goal(d)}
 
     obs_copy = pltpu.make_async_copy(obs_hbm.at[0, 0], obs, obs_sem)
     obs_copy.start()
@@ -144,7 +154,7 @@
         low[...] = l
 
     def forward(b, d):
-        base = lax.rem(s + slots - d, slots) * share
+        base = source(d) * share
 
         @pl.loop(0, share // 8)
         def _(i):
@@ -161,16 +171,19 @@
             mid[:, at, :] = z.reshape(wide, 8, nz)
 
     def middle():
-        @pl.loop(0, wide)
-        def _(r):
-            row = t * rows - rad + r
-            inside = jnp.logical_and(row >= 0, row < tiles * rows)
-            blurred = dot3((wy[0], wy[1]), split(mid[r]))
-            quotient = jnp.where(inside, obs[r], 0.0) / blurred
-            mid[r] = dot3((wyt[0], wyt[1]), split(quotient))
+        @pl.loop(0, wide // 2)
+        def _(i):
+            quotients = []
+            for r in (2 * i, 2 * i + 1):
+                row = t * rows - rad + r
+                inside = jnp.logical_and(row >= 0, row < tiles * rows)
+                blurred = dot3((wy[0], wy[1]), split(mid[r]))
+                quotients.append(jnp.where(inside, obs[r], 0.0) / blurred)
+            for r, quotient in zip((2 * i, 2 * i + 1), quotients):
+                mid[r] = dot3((wyt[0], wyt[1]), split(quotient))
 
     def backward(d, put):
-        base = lax.rem(s + d, slots) * share
+        base = goal(d) * share
 
         @pl.loop(0, share // 8)
         def _(i):
@@ -186,67 +199,155 @@
             z = dot3(data, (wz[0], wz[1])).reshape(rows, 8, nz) * scale[None]
             put(pl.ds(pl.multiple_of(i * 8, 8), 8), z)
 
+    def relayed(b, j, arriving=False):
+        whose = ((1, 2, 1, 2, 3, 3) if arriving else (0, 0, 0, 0, 1, 2))[j]
+        low = j in (0, 3, 4)
+        at = cells.at[b, pl.ds(2 * rad + (0 if low else half), half), cols(whose), :]
+        from_input = b == 0 and not arriving and whose == 0
+        return pltpu.make_async_remote_copy(
+            src_ref=est.at[pl.ds(0 if low else half, half)] if from_input else at,
+            dst_ref=at,
+            send_sem=gs.at[b, j], recv_sem=gr.at[b, j],
+            device_id=peer(1 if j in (0, 2, 5) else 2), device_id_type=pl.DeviceIdType.MESH,
+        )
+
+    def summed(b, j):
+        source, target, low = ((2, 2, 1), (2, 2, 0), (0, 0, 1), (1, 1, 0), (1, 1, 1), (0, 0, 0))[j]
+        part = pl.ds(0 if low else half, half)
+        return pltpu.make_async_remote_copy(
+            src_ref=sent.at[b, source, part], dst_ref=got.at[b, target, part],
+            send_sem=rs.at[b, j], recv_sem=rr.at[b, j],
+            device_id=peer(1 if j in (0, 2, 5) else 2), device_id_type=pl.DeviceIdType.MESH,
+        )
+
+    def combine(b, source, first):
+        @pl.loop(first, first + half)
+        def _(r):
+            sent[b, source, r] = sent[b, source, r] + got[b, 2, r]
+
+    def update(b, first, count, parts):
+        @pl.loop(first, first + count)
+        def _(r):
+            total = own[r]
+            for d in range(parts):
+                total = total + got[b, d, r]
+            new = cells[b, 2 * rad + r, cols(0), :] * total
+            if b == ITERS - 1:
+                out[r] = new
+            else:
+                cells[b + 1, 2 * rad + r, cols(0), :] = new
+
+    def keep(at, z):
+        own[:, at, :] = z
+
+    def fill(b):
+        @pl.when(jnp.logical_not(has_prev))
+        def _():
+            cells[b, pl.ds(0, 2 * rad), :, :] = jnp.zeros((2 * rad, ny, nz), jnp.float32)
+
+        @pl.when(jnp.logical_not(has_next))
+        def _():
+            cells[b, pl.ds(rows + 2 * rad, 2 * rad), :, :] = jnp.zeros((2 * rad, ny, nz), jnp.float32)
+
+    def prepare():
+        cells[0, pl.ds(2 * rad, rows), cols(0), :] = est[...]
+
+    def bands():
+        band(nz, 2, shift, wzt.at[0], wzt.at[1], True)
+        band(nz, 2, shift, wz.at[0], wz.at[1], False)
+        band(ny, 1, 0, wy.at[0], wy.at[1], False)
+        band(ny, 1, 0, wyt.at[0], wyt.at[1], True)
+
+    def send_back(b, d):
+        def put(at, z):
+            sent[b, d - 1, :, at, :] = z
+
+        backward(d, put)
+
     for b in range(ITERS):
-        for d in range(1, slots):
-            gather(b, d).start()
-        if b == 0:
-            cells[0, pl.ds(2 * rad, rows), cols(0), :] = est[...]
-        halo_start(b, 0)
-
-        @pl.when(jnp.logical_not(has_prev))
-        def _():
-            cells[b, pl.ds(0, 2 * rad), :, :] = jnp.zeros((2 * rad, ny, nz), jnp.float32)
-
-        @pl.when(jnp.logical_not(has_next))
-        def _():
-            cells[b, pl.ds(rows + 2 * rad, 2 * rad), :, :] = jnp.zeros((2 * rad, ny, nz), jnp.float32)
-
-        if b == 0:
-            band(nz, 2, shift, wzt.at[0], wzt.at[1], True)
-            band(nz, 2, shift, wz.at[0], wz.at[1], False)
-            band(ny, 1, 0, wy.at[0], wy.at[1], False)
-            band(ny, 1, 0, wyt.at[0], wyt.at[1], True)
-        for d in range(1, slots + 1):
-            if d < slots:
-                gather_in(b, d).wait_recv()
-                halo_start(b, d)
-            halo_wait(b, d - 1)
-            forward(b, d - 1)
+        if grid:
+            if b == 0:
+                for j in range(4):
+                    relayed(b, j).start()
+                prepare()
+            halo_start(b, 0)
+            fill(b)
+            if b == 0:
+                bands()
+            for j in range(2):
+                relayed(b, j, True).wait_recv()
+                relayed(b, 4 + j).start()
+            for j in range(2, 4):
+                relayed(b, j, True).wait_recv()
+                halo_start(b, j - 1)
+            halo_wait(b, 0)
+            forward(b, 0)
+            relayed(b, 4, True).wait_recv()
+            relayed(b, 5, True).wait_recv()
+            halo_start(b, 3)
+            for d in range(1, 4):
+                halo_wait(b, d)
+                forward(b, d)
+        else:
+            for d in range(1, slots):
+                gather(b, d).start()
+            if b == 0:
+                prepare()
+            halo_start(b, 0)
+            fill(b)
+            if b == 0:
+                bands()
+            for d in range(1, slots + 1):
+                if d < slots:
+                    gather_in(b, d).wait_recv()
+                    halo_start(b, d)
+                halo_wait(b, d - 1)
+                forward(b, d - 1)
         if b == 0:
             obs_copy.wait()
         middle()
-        for d in range(1, slots):
-            def put(at, z, d=d):
-                sent[b, d - 1, :, at, :] = z
-
-            backward(d, put)
-            scatter(b, d).start()
-
-        def keep(at, z):
-            own[:, at, :] = z
-
-        backward(0, keep)
-        for d in range(1, slots):
-            scatter(b, d).wait_recv()
-        target = out if b == ITERS - 1 else None
-
-        @pl.loop(0, rows)
-        def _(r):
-            total = own[r]
+        if grid:
+            send_back(b, 3)
+            summed(b, 0).start()
+            summed(b, 1).start()
+            send_back(b, 1)
+            summed(b, 2).start()
+            send_back(b, 2)
+            summed(b, 3).start()
+            summed(b, 0).wait_recv()
+            combine(b, 1, 0)
+            summed(b, 4).start()
+            summed(b, 1).wait_recv()
+            combine(b, 0, half)
+            summed(b, 5).start()
+            backward(0, keep)
+            for first, waits, starts in ((0, (2, 4), (0, 3)), (half, (3, 5), (1, 2))):
+                for j in waits:
+                    summed(b, j).wait_recv()
+                update(b, first, half, 2)
+                if b < ITERS - 1:
+                    for j in starts:
+                        relayed(b + 1, j).start()
+        else:
             for d in range(1, slots):
-                total = total + got[b, d - 1, r]
-            new = cells[b, 2 * rad + r, cols(0), :] * total
-            if target is not None:
-                out[r] = new
-            else:
-                cells[b + 1, 2 * rad + r, cols(0), :] = new
+                send_back(b, d)
+                scatter(b, d).start()
+            backward(0, keep)
+            for d in range(1, slots):
+                scatter(b, d).wait_recv()
+            update(b, 0, rows, slots - 1)
 
     for b in range(ITERS):
         for d in range(slots):
-            if d:
+            halo_sent(b, d)
+        if grid:
+            for j in range(6):
+                relayed(b, j).wait_send()
+                summed(b, j).wait_send()
+        else:
+            for d in range(1, slots):
                 gather(b, d).wait_send()
                 scatter(b, d).wait_send()
-            halo_sent(b, d)
 
 
 def per_device(tiles, slots, estimate, observed, psf, cover, offsets):
@@ -272,9 +373,9 @@
             pltpu.VMEM((2, ny, ny), bf16),
             pltpu.VMEM((2, ny, ny), bf16),
             dma,
-            dma((ITERS, slots)), dma((ITERS, slots)),
+            dma((ITERS, slots + 2)), dma((ITERS, slots + 2)),
             dma((ITERS, slots, 2)), dma((ITERS, slots, 2)),
-            dma((ITERS, slots)), dma((ITERS, slots)),
+            dma((ITERS, slots + 2)), dma((ITERS, slots + 2)),
         ],
         compiler_params=pltpu.CompilerParams(
             collective_id=0, has_side_effects=True, vmem_limit_bytes=48 * 1024 * 1024

time: 150 us -> 116 us (0.77)
  Pallas kernels: 143 us -> 109 us
    pallas_call x1, Pallas kernels: 143 us -> 109 us  [per_device(): pl.pallas_call(functools.partial(kernel, tiles, slots), out_shape=jax.Sha...]
where the time goes in v2:
time: 116 us; the launch traced here: 115 us
  Pallas kernels  109 us (94%)
  local copies, waits for them, and re-layouts  6.15 us (5%)
    pallas_call x1, Pallas kernels, per_device(): pl.pallas_call(functools.partial(kernel, tiles, slots), out_shape=jax.Sha...  109 us
    unnamed x8, local copies, waits for them, and re-layouts  6.15 us

profile of v2, /device:TPU:9, one launch (start us, length us, event | category | flops | bytes accessed | tf_op | source)
XLA Modules:
  0.0 114.8 jit_solution(1034356871099858510)
XLA Ops:
  0.0 0.8 copy.7.cover
  0.8 0.8 copy.8.offsets
  1.5 0.8 copy.6.psf
  2.3 0.0 copy-start
  2.4 2.0 %copy-done = f32[1,1,26,128,256]{4,3,2,1,0:T(8,128)S(1)} copy-done((f32[1,1,26,128,256]{4,3,2,1,0:T(8,128)S(1)}, f32[1,1,26,128,256]{4,3,2,1,0:T(8,128)}, u32[]{:S(2)}) %copy-start) | copy-done | bytes 3407896
  4.3 0.0 copy-start.1
  4.3 1.0 copy-done.1
  5.4 108.7 %shard_map.55 = f32[16,32,256]{2,1,0:T(8,128)S(1)} custom-call(f32[16,32,256]{2,1,0:T(8,128)S(1)} %copy-done.1, f32[1,1,26,128,256]{4,3,2,1,0:T(8,128)S(1)} %copy-done, f32[12,3,11]{2,1,0:T(4,128)S(1)} %copy.6.psf, s32[8,4]{1,0:T(8,128)S(1)} %copy.7.cover, s32[8,4]{1,0:T(8,128)S(1)} %copy.8.offsets), custom_call_target="tpu_custom_call" | custom-call | tf_op jit(solution)/shard_map/pallas_call | solution.py:359
  114.0 0.8 copy.10
Async XLA Ops:
  2.3 2.0 %copy-start = (f32[1,1,26,128,256]{4,3,2,1,0:T(8,128)S(1)}, f32[1,1,26,128,256]{4,3,2,1,0:T(8,128)}, u32[]{:S(2)}) copy-start(f32[1,1,26,128,256]{4,3,2,1,0:T(8,128)} %obs_hbm.1) | copy-start | bytes 10223620
  4.3 1.0 copy-start.1

commit v3 on v2

--- a/solution.py
+++ b/solution.py
@@ -28,19 +28,19 @@
 def kernel(
     tiles, slots, est, obs_hbm, psf, cover, offsets, out,
     cells, mid, obs, sent, got, own, wz, wzt, wy, wyt,
-    obs_sem, gs, gr, hs, hr, rs, rr,
+    obs_sem, est_sem, gs, gr, hs, hr, rs, rr,
 ):
     t = lax.axis_index("tile")
     s = lax.axis_index("view")
     rows, share, nz = est.shape
     ny = mid.shape[1]
-    views, _, taps = psf.shape
+    taps, _, views = psf.shape
     rad = taps // 2
     wide = rows + 2 * rad
     has_prev, has_next = t > 0, t < tiles - 1
 
-    half = rows // 2
-    grid = slots == 4
+    half, chunk = share // 2, rows // 2
+    grid = slots == 4 and share % 16 == 0
     around = (s, s + 1 - 2 * lax.rem(s, 2), lax.rem(s + 2, 4), 3 - s)
 
     def source(d):
@@ -56,6 +56,8 @@
         return {"view": goal(d)}
 
     obs_copy = pltpu.make_async_copy(obs_hbm.at[0, 0], obs, obs_sem)
+    est_copy = pltpu.make_async_copy(est, cells.at[0, pl.ds(2 * rad, rows), cols(0), :], est_sem)
+    est_copy.start()
     obs_copy.start()
 
     barrier = pltpu.get_barrier_semaphore()
@@ -78,7 +80,7 @@
         return pltpu.make_async_remote_copy(
             src_ref=src,
             dst_ref=cells.at[b, pl.ds(2 * rad, rows), cols(0), :],
-            send_sem=gs.at[b, d], recv_sem=gr.at[b, d],
+            send_sem=gs.at[b, 0, d], recv_sem=gr.at[b, 0, d],
             device_id=peer(d), device_id_type=pl.DeviceIdType.MESH,
         )
 
@@ -86,7 +88,7 @@
         block = cells.at[b, pl.ds(2 * rad, rows), cols(d), :]
         return pltpu.make_async_remote_copy(
             src_ref=block, dst_ref=block,
-            send_sem=gs.at[b, d], recv_sem=gr.at[b, d],
+            send_sem=gs.at[b, 0, d], recv_sem=gr.at[b, 0, d],
             device_id=peer(d), device_id_type=pl.DeviceIdType.MESH,
         )
 
@@ -129,18 +131,18 @@
     def scatter(b, d):
         return pltpu.make_async_remote_copy(
             src_ref=sent.at[b, d - 1], dst_ref=got.at[b, d - 1],
-            send_sem=rs.at[b, d], recv_sem=rr.at[b, d],
+            send_sem=rs.at[b, 0, d], recv_sem=rr.at[b, 0, d],
             device_id=peer(d), device_id_type=pl.DeviceIdType.MESH,
         )
 
-    view = cover[t, s]
+    view = cover[s, t]
     clipped = jnp.minimum(view, views - 1)
-    shift = offsets[t, s]
+    shift = offsets[s, t]
     count = jnp.float32(0.0)
     for d in range(slots):
-        count = count + jnp.where(cover[t, d] < views, 1.0, 0.0)
+        count = count + jnp.where(cover[d, t] < views, 1.0, 0.0)
     scale = jnp.where(view < views, 1.0, 0.0) / jnp.full((8, nz), count, jnp.float32)
-    bx = [psf[clipped, 0, k] for k in range(taps)]
+    bx = [psf[k, 0, clipped] for k in range(taps)]
 
     def band(size, axis, offset, high, low, transposed):
         r = lax.broadcasted_iota(jnp.int32, (size, size), 1 if transposed else 0)
@@ -148,7 +150,7 @@
         where = c - r - offset + rad
         weight = jnp.zeros((size, size), jnp.float32)
         for k in range(taps):
-            weight = jnp.where(where == k, psf[clipped, axis, k], weight)
+            weight = jnp.where(where == k, psf[k, axis, clipped], weight)
         h, l = split(weight)
         high[...] = h
         low[...] = l
@@ -170,8 +172,8 @@
             z = dot3(data, (wzt[0], wzt[1]))
             mid[:, at, :] = z.reshape(wide, 8, nz)
 
-    def middle():
-        @pl.loop(0, wide // 2)
+    def middle(begin, end):
+        @pl.loop(begin, end)
         def _(i):
             quotients = []
             for r in (2 * i, 2 * i + 1):
@@ -182,48 +184,53 @@
             for r, quotient in zip((2 * i, 2 * i + 1), quotients):
                 mid[r] = dot3((wyt[0], wyt[1]), split(quotient))
 
-    def backward(d, put):
+    step = 16 if grid else 8
+
+    def backward(d, put, first, number):
         base = goal(d) * share
 
-        @pl.loop(0, share // 8)
+        @pl.loop(0, share // step)
         def _(i):
-            at = pl.ds(pl.multiple_of(base + i * 8, 8), 8)
-            q = [mid[j, at, :] for j in range(wide)]
+            at = pl.ds(pl.multiple_of(base + i * step, 8), step)
+            q = [mid[first + j, at, :] for j in range(number + 2 * rad)]
             sums = []
-            for r in range(rows):
+            for r in range(number):
                 total = bx[0] * q[r + 2 * rad]
                 for k in range(1, taps):
                     total = total + bx[k] * q[r + 2 * rad - k]
                 sums.append(total)
             data = split(jnp.concatenate(sums, axis=0))
-            z = dot3(data, (wz[0], wz[1])).reshape(rows, 8, nz) * scale[None]
-            put(pl.ds(pl.multiple_of(i * 8, 8), 8), z)
-
-    def relayed(b, j, arriving=False):
+            z = dot3(data, (wz[0], wz[1])) * scale[0:1]
+            put(pl.ds(first, number), pl.ds(pl.multiple_of(i * step, 8), step), z.reshape(number, step, nz))
+
+    def relayed(b, c, j, arriving=False):
         whose = ((1, 2, 1, 2, 3, 3) if arriving else (0, 0, 0, 0, 1, 2))[j]
-        low = j in (0, 3, 4)
-        at = cells.at[b, pl.ds(2 * rad + (0 if low else half), half), cols(whose), :]
+        side = 0 if j in (0, 3, 4) else half
+        columns = pl.ds(pl.multiple_of(source(whose) * share + side, 8), half)
+        at = cells.at[b, pl.ds(2 * rad + c * chunk, chunk), columns, :]
         from_input = b == 0 and not arriving and whose == 0
         return pltpu.make_async_remote_copy(
-            src_ref=est.at[pl.ds(0 if low else half, half)] if from_input else at,
+            src_ref=est.at[pl.ds(c * chunk, chunk), pl.ds(side, half), :] if from_input else at,
             dst_ref=at,
-            send_sem=gs.at[b, j], recv_sem=gr.at[b, j],
+            send_sem=gs.at[b, c, j], recv_sem=gr.at[b, c, j],
             device_id=peer(1 if j in (0, 2, 5) else 2), device_id_type=pl.DeviceIdType.MESH,
         )
 
-    def summed(b, j):
-        source, target, low = ((2, 2, 1), (2, 2, 0), (0, 0, 1), (1, 1, 0), (1, 1, 1), (0, 0, 0))[j]
-        part = pl.ds(0 if low else half, half)
-        return pltpu.make_async_remote_copy(
-            src_ref=sent.at[b, source, part], dst_ref=got.at[b, target, part],
-            send_sem=rs.at[b, j], recv_sem=rr.at[b, j],
+    def summed(b, c, j):
+        origin, target, side = ((2, 2, 0), (2, 2, half), (0, 0, 0), (1, 1, half), (1, 1, 0), (0, 0, half))[j]
+        part = (pl.ds(c * chunk, chunk), pl.ds(side, half))
+        return pltpu.make_async_remote_copy(
+            src_ref=sent.at[b, origin, *part], dst_ref=got.at[b, target, *part],
+            send_sem=rs.at[b, c, j], recv_sem=rr.at[b, c, j],
             device_id=peer(1 if j in (0, 2, 5) else 2), device_id_type=pl.DeviceIdType.MESH,
         )
 
-    def combine(b, source, first):
-        @pl.loop(first, first + half)
-        def _(r):
-            sent[b, source, r] = sent[b, source, r] + got[b, 2, r]
+    def combine(b, c):
+        for j, origin, side in ((0, 1, 0), (1, 0, half)):
+            summed(b, c, j).wait_recv()
+            part = (pl.ds(c * chunk, chunk), pl.ds(side, half))
+            sent[b, origin, *part] = sent[b, origin, *part] + got[b, 2, *part]
+            summed(b, c, 4 + j).start()
 
     def update(b, first, count, parts):
         @pl.loop(first, first + count)
@@ -237,8 +244,8 @@
             else:
                 cells[b + 1, 2 * rad + r, cols(0), :] = new
 
-    def keep(at, z):
-        own[:, at, :] = z
+    def keep(part, at, z):
+        own[part, at, :] = z
 
     def fill(b):
         @pl.when(jnp.logical_not(has_prev))
@@ -250,7 +257,7 @@
             cells[b, pl.ds(rows + 2 * rad, 2 * rad), :, :] = jnp.zeros((2 * rad, ny, nz), jnp.float32)
 
     def prepare():
-        cells[0, pl.ds(2 * rad, rows), cols(0), :] = est[...]
+        est_copy.wait()
 
     def bands():
         band(nz, 2, shift, wzt.at[0], wzt.at[1], True)
@@ -258,32 +265,36 @@
         band(ny, 1, 0, wy.at[0], wy.at[1], False)
         band(ny, 1, 0, wyt.at[0], wyt.at[1], True)
 
-    def send_back(b, d):
-        def put(at, z):
-            sent[b, d - 1, :, at, :] = z
-
-        backward(d, put)
+    def send_back(b, d, first, number):
+        def put(part, at, z):
+            sent[b, d - 1, part, at, :] = z
+
+        backward(d, put, first, number)
 
     for b in range(ITERS):
         if grid:
             if b == 0:
-                for j in range(4):
-                    relayed(b, j).start()
+                for c in range(2):
+                    for j in range(4):
+                        relayed(b, c, j).start()
                 prepare()
             halo_start(b, 0)
             fill(b)
             if b == 0:
                 bands()
-            for j in range(2):
-                relayed(b, j, True).wait_recv()
-                relayed(b, 4 + j).start()
+            for c in range(2):
+                for j in range(2):
+                    relayed(b, c, j, True).wait_recv()
+                    relayed(b, c, 4 + j).start()
             for j in range(2, 4):
-                relayed(b, j, True).wait_recv()
+                for c in range(2):
+                    relayed(b, c, j, True).wait_recv()
                 halo_start(b, j - 1)
             halo_wait(b, 0)
             forward(b, 0)
-            relayed(b, 4, True).wait_recv()
-            relayed(b, 5, True).wait_recv()
+            for c in range(2):
+                relayed(b, c, 4, True).wait_recv()
+                relayed(b, c, 5, True).wait_recv()
             halo_start(b, 3)
             for d in range(1, 4):
                 halo_wait(b, d)
@@ -305,34 +316,32 @@
                 forward(b, d - 1)
         if b == 0:
             obs_copy.wait()
-        middle()
         if grid:
-            send_back(b, 3)
-            summed(b, 0).start()
-            summed(b, 1).start()
-            send_back(b, 1)
-            summed(b, 2).start()
-            send_back(b, 2)
-            summed(b, 3).start()
-            summed(b, 0).wait_recv()
-            combine(b, 1, 0)
-            summed(b, 4).start()
-            summed(b, 1).wait_recv()
-            combine(b, 0, half)
-            summed(b, 5).start()
-            backward(0, keep)
-            for first, waits, starts in ((0, (2, 4), (0, 3)), (half, (3, 5), (1, 2))):
-                for j in waits:
-                    summed(b, j).wait_recv()
-                update(b, first, half, 2)
+            ready = (chunk + 2 * rad + 1) // 2
+            for c, begin, end in ((0, 0, ready), (1, ready, wide // 2)):
+                middle(begin, end)
+                if c == 1:
+                    combine(b, 0)
+                for d, copies in ((3, (0, 1)), (1, (2,)), (2, (3,))):
+                    send_back(b, d, c * chunk, chunk)
+                    for j in copies:
+                        summed(b, c, j).start()
+            backward(0, keep, 0, chunk)
+            combine(b, 1)
+            backward(0, keep, chunk, chunk)
+            for c in range(2):
+                for j in range(2, 6):
+                    summed(b, c, j).wait_recv()
+                update(b, c * chunk, chunk, 2)
                 if b < ITERS - 1:
-                    for j in starts:
-                        relayed(b + 1, j).start()
+                    for j in range(4):
+                        relayed(b + 1, c, j).start()
         else:
+            middle(0, wide // 2)
             for d in range(1, slots):
-                send_back(b, d)
+                send_back(b, d, 0, rows)
                 scatter(b, d).start()
-            backward(0, keep)
+            backward(0, keep, 0, rows)
             for d in range(1, slots):
                 scatter(b, d).wait_recv()
             update(b, 0, rows, slots - 1)
@@ -341,9 +350,10 @@
         for d in range(slots):
             halo_sent(b, d)
         if grid:
-            for j in range(6):
-                relayed(b, j).wait_send()
-                summed(b, j).wait_send()
+            for c in range(2):
+                for j in range(6):
+                    relayed(b, c, j).wait_send()
+                    summed(b, c, j).wait_send()
         else:
             for d in range(1, slots):
                 gather(b, d).wait_send()
@@ -359,7 +369,7 @@
     return pl.pallas_call(
         functools.partial(kernel, tiles, slots),
         out_shape=jax.ShapeDtypeStruct(estimate.shape, f32),
-        in_specs=[vmem, pl.BlockSpec(memory_space=pl.ANY), smem, smem, smem],
+        in_specs=[pl.BlockSpec(memory_space=pl.ANY)] * 2 + [smem] * 3,
         out_specs=vmem,
         scratch_shapes=[
             pltpu.VMEM((ITERS, 2 * wide - rows, ny, nz), f32),
@@ -372,15 +382,15 @@
             pltpu.VMEM((2, nz, nz), bf16),
             pltpu.VMEM((2, ny, ny), bf16),
             pltpu.VMEM((2, ny, ny), bf16),
-            dma,
-            dma((ITERS, slots + 2)), dma((ITERS, slots + 2)),
+            dma, dma,
+            dma((ITERS, 2, slots + 2)), dma((ITERS, 2, slots + 2)),
             dma((ITERS, slots, 2)), dma((ITERS, slots, 2)),
-            dma((ITERS, slots + 2)), dma((ITERS, slots + 2)),
+            dma((ITERS, 2, slots + 2)), dma((ITERS, 2, slots + 2)),
         ],
         compiler_params=pltpu.CompilerParams(
-            collective_id=0, has_side_effects=True, vmem_limit_bytes=48 * 1024 * 1024
+            collective_id=0, has_side_effects=True, vmem_limit_bytes=60 * 1024 * 1024
         ),
-    )(estimate, observed, psf, cover, offsets)
+    )(estimate, observed, psf.transpose(2, 1, 0), cover.T, offsets.T)
 
 
 def solution(mesh):

time: 116 us -> 108 us (0.931)
  local copies, waits for them, and re-layouts: 6.15 us -> 1.88 us
  Pallas kernels: 109 us -> 106 us
    unnamed x8 -> x1, local copies, waits for them, and re-layouts: 6.15 us -> 1.88 us
    pallas_call x1, Pallas kernels: 109 us -> 106 us  [per_device(): pl.pallas_call(functools.partial(kernel, tiles, slots), out_shape=jax.Sha...]
where the time goes in v3:
time: 108 us
  Pallas kernels  106 us (98%)
  local copies, waits for them, and re-layouts  1.88 us (2%)
    pallas_call x1, Pallas kernels, per_device(): pl.pallas_call(functools.partial(kernel, tiles, slots), out_shape=jax.Sha...  106 us

profile of v3, /device:TPU:9, one launch (start us, length us, event | category | flops | bytes accessed | tf_op | source)
XLA Modules:
  0.0 107.8 jit_solution(13594558110405652536)
XLA Ops:
  0.0 105.9 %shard_map.55 = f32[16,32,256]{2,1,0:T(8,128)} custom-call(f32[16,32,256]{2,1,0:T(8,128)} %est.1, f32[1,1,26,128,256]{4,3,2,1,0:T(8,128)} %obs_hbm.1, f32[11,3,12]{2,1,0:T(4,128)} %bitcast.3, s32[4,8]{1,0:T(4,128)} %bitcast.4, s32[4,8]{1,0:T(4,128)} %bitcast.5), custom_call_target="tpu_custom_call" | custom-call | tf_op jit(solution)/shard_map/pallas_call | solution.py:369
  106.0 1.9 %copy.7 = f32[16,32,256]{2,1,0:T(8,128)} copy(f32[16,32,256]{2,1,0:T(8,128)} %shard_map.55) | data formatting | bytes 1048576

commit v4 on v3

--- a/solution.py
+++ b/solution.py
@@ -158,9 +158,9 @@
     def forward(b, d):
         base = source(d) * share
 
-        @pl.loop(0, share // 8)
+        @pl.loop(0, share // step)
         def _(i):
-            at = pl.ds(pl.multiple_of(base + i * 8, 8), 8)
+            at = pl.ds(pl.multiple_of(base + i * step, 8), step)
             x = [cells[b, j, at, :] for j in range(rows + 4 * rad)]
             sums = []
             for r in range(wide):
@@ -170,7 +170,7 @@
                 sums.append(total)
             data = split(jnp.concatenate(sums, axis=0))
             z = dot3(data, (wzt[0], wzt[1]))
-            mid[:, at, :] = z.reshape(wide, 8, nz)
+            mid[:, at, :] = z.reshape(wide, step, nz)
 
     def middle(begin, end):
         @pl.loop(begin, end)

time: 108 us -> 106 us (0.981)
  Pallas kernels: 106 us -> 104 us
    pallas_call x1, Pallas kernels: 106 us -> 104 us  [per_device(): pl.pallas_call(functools.partial(kernel, tiles, slots), out_shape=jax.Sha...]
where the time goes in v4:
time: 106 us
  Pallas kernels  104 us (98%)
  local copies, waits for them, and re-layouts  1.88 us (2%)
    pallas_call x1, Pallas kernels, per_device(): pl.pallas_call(functools.partial(kernel, tiles, slots), out_shape=jax.Sha...  104 us

profile of v4, /device:TPU:9, one launch (start us, length us, event | category | flops | bytes accessed | tf_op | source)
XLA Modules:
  0.0 106.1 jit_solution(892806551834550217)
XLA Ops:
  0.0 104.2 %shard_map.55 = f32[16,32,256]{2,1,0:T(8,128)} custom-call(f32[16,32,256]{2,1,0:T(8,128)} %est.1, f32[1,1,26,128,256]{4,3,2,1,0:T(8,128)} %obs_hbm.1, f32[11,3,12]{2,1,0:T(4,128)} %bitcast.3, s32[4,8]{1,0:T(4,128)} %bitcast.4, s32[4,8]{1,0:T(4,128)} %bitcast.5), custom_call_target="tpu_custom_call" | custom-call | tf_op jit(solution)/shard_map/pallas_call | solution.py:369
  104.2 1.9 %copy.7 = f32[16,32,256]{2,1,0:T(8,128)} copy(f32[16,32,256]{2,1,0:T(8,128)} %shard_map.55) | data formatting | bytes 1048576
